TPU v7x, 32 devices: a whole 2x2x4 slice. The times are simulated.
32 devices in a mesh: dp: 4 (over y, core), fsdp: 8 (over z, x).
Axes of the slice: x: 2, y: 2, z: 4, core: 2. Of those that a mesh axis runs over, the one named last changes fastest.
Arguments:
- tokens: bfloat16 [16384, 768], P(('dp', 'fsdp')), may hold values from -6 to 6
- segment_ids: int32 [16384], P(('dp', 'fsdp')), may hold values from 0 to 3, as said below
- ln1_gain: bfloat16 [768], P(('dp', 'fsdp')), may hold values from 0.5 to 1.5
- ln1_bias: bfloat16 [768], P(('dp', 'fsdp')), may hold values from -1 to 1
- qkv_weight: bfloat16 [768, 2304], P(('dp', 'fsdp')), may hold values from -0.21875 to 0.21875
- qkv_bias: bfloat16 [2304], P(('dp', 'fsdp')), may hold values from -1 to 1
- out_weight: bfloat16 [768, 768], P(('dp', 'fsdp')), may hold values from -1.75 to 1.75
- out_bias: bfloat16 [768], P(('dp', 'fsdp')), may hold values from -1 to 1
- ln2_gain: bfloat16 [768], P(('dp', 'fsdp')), may hold values from 0.5 to 1.5
- ln2_bias: bfloat16 [768], P(('dp', 'fsdp')), may hold values from -1 to 1
- fc1_weight: bfloat16 [768, 3072], P(('dp', 'fsdp')), may hold values from -0.21875 to 0.21875
- fc1_bias: bfloat16 [3072], P(('dp', 'fsdp')), may hold values from -1 to 1
- fc2_weight: bfloat16 [3072, 768], P(('dp', 'fsdp')), may hold values from -0.109375 to 0.109375
- fc2_bias: bfloat16 [768], P(('dp', 'fsdp')), may hold values from -1 to 1
- output_grad: bfloat16 [16384, 768], P(('dp', 'fsdp')), may hold values from -6 to 6
Outputs:
- output: bfloat16 [16384, 768], P(('dp', 'fsdp'))
- input_grad: float32 [16384, 768], P(('dp', 'fsdp'))
- ln1_gain_grad: float32 [768], P(('dp', 'fsdp'))
- ln1_bias_grad: float32 [768], P(('dp', 'fsdp'))
- qkv_weight_grad: float32 [768, 2304], P(('dp', 'fsdp'))
- qkv_bias_grad: float32 [2304], P(('dp', 'fsdp'))
- out_weight_grad: float32 [768, 768], P(('dp', 'fsdp'))
- out_bias_grad: float32 [768], P(('dp', 'fsdp'))
- ln2_gain_grad: float32 [768], P(('dp', 'fsdp'))
- ln2_bias_grad: float32 [768], P(('dp', 'fsdp'))
- fc1_weight_grad: float32 [768, 3072], P(('dp', 'fsdp'))
- fc1_bias_grad: float32 [3072], P(('dp', 'fsdp'))
- fc2_weight_grad: float32 [3072, 768], P(('dp', 'fsdp'))
- fc2_bias_grad: float32 [768], P(('dp', 'fsdp'))
Inputs may be any that keep to these rules, and one draw needn't show every extreme that they name: `segment_ids`: within each sequence of 1024 tokens the numbers never fall and every one of 0, 1, 2, 3 occurs.
All inputs are finite; a program needn't handle non-finite values.
Results may differ from a plain program's by a relative error of at most 0.01.
Values may be sent and summed in bfloat16 or wider, within the bound.
No kernel may reach another device: no remote copies, remote signals or barrier semaphores. Data moves between devices by JAX's collectives and lax.ppermute only.
A program may use at most 192 MiB of HBM per device.

v0:
```python
import jax
import jax.numpy as jnp
from jax import lax
from jax.sharding import PartitionSpec as P

D = 768
HEAD = 64


EPSILON = 1e-05


def from_behind(block, axis, distance):
    devices = range(lax.axis_size(axis))
    route = [(i - distance, i) for i in devices if i - distance in devices]
    return lax.ppermute(block, axis, route)


def layer_norm(inputs, gain_vec, bias_vec):
    average = jnp.mean(inputs, -1, keepdims=True)
    centred = inputs - average
    spread = jnp.mean(centred * centred, -1, keepdims=True)
    return centred * lax.rsqrt(spread + EPSILON) * gain_vec + bias_vec


def split_heads(matrix):
    return matrix.reshape(matrix.shape[0], -1, 4, HEAD).transpose(1, 0, 2, 3)


def merge_heads(stacked):
    return stacked.transpose(1, 0, 2, 3).reshape(stacked.shape[1], -1)


def score_tile(queries, key_rows):
    return jnp.einsum(
        "rhe,khe->hrk", queries, key_rows, preferred_element_type=jnp.float32
    ) * HEAD ** (-0.5)


def forward_tile(queries, key_rows, value_rows, allowed):
    scores = score_tile(queries, key_rows)
    magnitude = jnp.sqrt(scores * scores + 1.0)
    row_max = jnp.max(jnp.where(allowed, magnitude, -1e30), -1, keepdims=True)
    raised = jnp.where(allowed, jnp.exp(magnitude - row_max), 0.0)
    totals = jnp.sum(raised, -1, keepdims=True)
    attention = (scores / magnitude * (raised / totals)).astype(jnp.bfloat16)
    mixture = jnp.einsum("hrk,khe->rhe", attention, value_rows, preferred_element_type=jnp.float32)
    return (mixture, (row_max + jnp.log(totals))[..., 0])


def backward_tile(queries, key_rows, value_rows, mix_grad, log_total, allowed):
    scores = score_tile(queries, key_rows)
    magnitude = jnp.sqrt(scores * scores + 1.0)
    signs = scores / magnitude
    probs = jnp.where(allowed, jnp.exp(magnitude - log_total[..., None]), 0.0)
    attention = (signs * probs).astype(jnp.bfloat16)
    weight_grad = jnp.einsum(
        "rhe,khe->hrk", mix_grad, value_rows, preferred_element_type=jnp.float32
    )
    centre = jnp.sum(probs * signs * weight_grad, -1, keepdims=True)
    score_grad = probs * signs * (signs * weight_grad - centre) + probs * weight_grad / (
        magnitude * magnitude * magnitude
    )
    score_grad = score_grad.astype(jnp.bfloat16)
    value_grad = jnp.einsum("hrk,rhe->khe", attention, mix_grad, preferred_element_type=jnp.float32)
    query_grad = jnp.einsum(
        "hrk,khe->rhe", score_grad, key_rows, preferred_element_type=jnp.float32
    ) * HEAD ** (-0.5)
    key_grad = jnp.einsum(
        "hrk,rhe->khe", score_grad, queries, preferred_element_type=jnp.float32
    ) * HEAD ** (-0.5)
    return (query_grad, key_grad, value_grad)


def visible(marks, prev_marks, later):
    row_count = marks.shape[0]
    position = jnp.arange(row_count, dtype=jnp.int32)
    own_part = (marks[:, None] == marks[None, :]) & (position[:, None] >= position[None, :])
    earlier = (marks[:, None] == prev_marks[None, :]) & later
    return jnp.concatenate([earlier, own_part], 1)


def project(inputs, attn_full):
    normed = layer_norm(
        inputs, attn_full[0].astype(jnp.float32), attn_full[1].astype(jnp.float32)
    ).astype(jnp.bfloat16)
    packed = (
        jnp.dot(normed, attn_full[2], preferred_element_type=jnp.float32)
        + attn_full[3].astype(jnp.float32)
    ).astype(jnp.bfloat16)
    return (normed, packed)


def attend(packed, kv_prev, allowed):
    queries = split_heads(packed[:, :D])
    key_rows = split_heads(jnp.concatenate([kv_prev[:, :D], packed[:, D : 2 * D]], 0))
    value_rows = split_heads(jnp.concatenate([kv_prev[:, D:], packed[:, 2 * D :]], 0))
    mixture, log_total = lax.map(
        lambda group_in: forward_tile(group_in[0], group_in[1], group_in[2], allowed),
        (queries, key_rows, value_rows),
    )
    return (merge_heads(mixture).astype(jnp.bfloat16), (queries, key_rows, value_rows, log_total))


def feed_forward(middle, mlp_full):
    normed = layer_norm(
        middle, mlp_full[0].astype(jnp.float32), mlp_full[1].astype(jnp.float32)
    ).astype(jnp.bfloat16)
    before = jnp.dot(normed, mlp_full[2], preferred_element_type=jnp.float32) + mlp_full[3].astype(
        jnp.float32
    )
    hidden = jax.nn.gelu(before).astype(jnp.bfloat16)
    result = (
        middle
        + jnp.dot(hidden, mlp_full[4], preferred_element_type=jnp.float32)
        + mlp_full[5].astype(jnp.float32)
    )
    return (normed, before, hidden, result)


def on_device(
    tokens,
    segment_ids,
    ln1_gain,
    ln1_bias,
    qkv_weight,
    qkv_bias,
    out_weight,
    out_bias,
    ln2_gain,
    ln2_bias,
    fc1_weight,
    fc1_bias,
    fc2_weight,
    fc2_bias,
    output_grad,
):
    later = lax.axis_index("fsdp") % 2 == 1
    inputs = tokens.astype(jnp.float32)
    marks = segment_ids.astype(jnp.bfloat16)
    row_count = tokens.shape[0]
    attn_full = (
        lax.all_gather(ln1_gain, ("dp", "fsdp"), axis=0, tiled=True),
        lax.all_gather(ln1_bias, ("dp", "fsdp"), axis=0, tiled=True),
        lax.all_gather(qkv_weight, ("dp", "fsdp"), axis=0, tiled=True),
        lax.all_gather(qkv_bias, ("dp", "fsdp"), axis=0, tiled=True),
        lax.all_gather(out_weight, ("dp", "fsdp"), axis=0, tiled=True),
        lax.all_gather(out_bias, ("dp", "fsdp"), axis=0, tiled=True),
    )
    packed = project(inputs, attn_full)[1]
    kv_prev, prev_marks = from_behind((packed[:, D:], marks), "fsdp", 1)
    allowed = visible(marks, prev_marks, later)
    mixture = attend(packed, kv_prev, allowed)[0]
    middle = (
        inputs
        + jnp.dot(mixture, attn_full[4], preferred_element_type=jnp.float32)
        + attn_full[5].astype(jnp.float32)
    )
    mlp_full = (
        lax.all_gather(ln2_gain, ("dp", "fsdp"), axis=0, tiled=True),
        lax.all_gather(ln2_bias, ("dp", "fsdp"), axis=0, tiled=True),
        lax.all_gather(fc1_weight, ("dp", "fsdp"), axis=0, tiled=True),
        lax.all_gather(fc1_bias, ("dp", "fsdp"), axis=0, tiled=True),
        lax.all_gather(fc2_weight, ("dp", "fsdp"), axis=0, tiled=True),
        lax.all_gather(fc2_bias, ("dp", "fsdp"), axis=0, tiled=True),
    )
    output = feed_forward(middle, mlp_full)[3].astype(jnp.bfloat16)
    mlp_back = (
        lax.all_gather(ln2_gain, ("dp", "fsdp"), axis=0, tiled=True),
        lax.all_gather(ln2_bias, ("dp", "fsdp"), axis=0, tiled=True),
        lax.all_gather(fc1_weight, ("dp", "fsdp"), axis=0, tiled=True),
        lax.all_gather(fc1_bias, ("dp", "fsdp"), axis=0, tiled=True),
        lax.all_gather(fc2_weight, ("dp", "fsdp"), axis=0, tiled=True),
        lax.all_gather(fc2_bias, ("dp", "fsdp"), axis=0, tiled=True),
    )
    recomputed = feed_forward(middle, mlp_back)
    normed_two, before, hidden = (recomputed[0], recomputed[1], recomputed[2])
    cotangent = output_grad.astype(jnp.float32)
    fc2_grad = jnp.einsum("rf,rd->fd", hidden, output_grad, preferred_element_type=jnp.float32)
    fc2_bias_grad = jnp.sum(cotangent, 0)
    hidden_grad = jnp.einsum(
        "rd,fd->rf", output_grad, mlp_back[4], preferred_element_type=jnp.float32
    )
    gelu_pull = jax.vjp(jax.nn.gelu, before)[1]
    before_grad = gelu_pull(hidden_grad)[0].astype(jnp.bfloat16)
    fc1_grad = jnp.einsum("rd,rf->df", normed_two, before_grad, preferred_element_type=jnp.float32)
    fc1_bias_grad = jnp.sum(before_grad.astype(jnp.float32), 0)
    normed_grad = jnp.einsum(
        "rf,df->rd", before_grad, mlp_back[2], preferred_element_type=jnp.float32
    )
    norm_pull = jax.vjp(
        layer_norm, middle, mlp_back[0].astype(jnp.float32), mlp_back[1].astype(jnp.float32)
    )[1]
    middle_part, ln2_gain_grad, ln2_bias_grad = norm_pull(normed_grad)
    middle_grad = cotangent + middle_part
    mlp_grads = (
        lax.psum_scatter(ln2_gain_grad, ("dp", "fsdp"), scatter_dimension=0, tiled=True),
        lax.psum_scatter(ln2_bias_grad, ("dp", "fsdp"), scatter_dimension=0, tiled=True),
        lax.psum_scatter(fc1_grad, ("dp", "fsdp"), scatter_dimension=0, tiled=True),
        lax.psum_scatter(fc1_bias_grad, ("dp", "fsdp"), scatter_dimension=0, tiled=True),
        lax.psum_scatter(fc2_grad, ("dp", "fsdp"), scatter_dimension=0, tiled=True),
        lax.psum_scatter(fc2_bias_grad, ("dp", "fsdp"), scatter_dimension=0, tiled=True),
    )
    attn_back = (
        lax.all_gather(ln1_gain, ("dp", "fsdp"), axis=0, tiled=True),
        lax.all_gather(ln1_bias, ("dp", "fsdp"), axis=0, tiled=True),
        lax.all_gather(qkv_weight, ("dp", "fsdp"), axis=0, tiled=True),
        lax.all_gather(qkv_bias, ("dp", "fsdp"), axis=0, tiled=True),
        lax.all_gather(out_weight, ("dp", "fsdp"), axis=0, tiled=True),
        lax.all_gather(out_bias, ("dp", "fsdp"), axis=0, tiled=True),
    )
    normed, packed = project(inputs, attn_back)
    kv_back, marks_back = from_behind((packed[:, D:], marks), "fsdp", 1)
    allowed_back = visible(marks, marks_back, later)
    mixture, saved = attend(packed, kv_back, allowed_back)
    queries, key_rows, value_rows, log_total = saved
    proj_grad = middle_grad.astype(jnp.bfloat16)
    out_grad = jnp.einsum("rd,re->de", mixture, proj_grad, preferred_element_type=jnp.float32)
    out_bias_grad = jnp.sum(middle_grad, 0)
    mix_grad = split_heads(
        jnp.einsum("re,de->rd", proj_grad, attn_back[4], preferred_element_type=jnp.float32).astype(
            jnp.bfloat16
        )
    )
    tile_grads = lax.map(
        lambda group_in: backward_tile(
            group_in[0], group_in[1], group_in[2], group_in[3], group_in[4], allowed_back
        ),
        (queries, key_rows, value_rows, mix_grad, log_total),
    )
    query_grad = merge_heads(tile_grads[0])
    key_grad = merge_heads(tile_grads[1])
    value_grad = merge_heads(tile_grads[2])
    returned = from_behind(
        jnp.concatenate([key_grad[:row_count], value_grad[:row_count]], 1).astype(jnp.bfloat16),
        "fsdp",
        -1,
    ).astype(jnp.float32)
    kv_grad = jnp.concatenate([key_grad[row_count:], value_grad[row_count:]], 1) + returned
    packed_grad = jnp.concatenate([query_grad, kv_grad], 1).astype(jnp.bfloat16)
    qkv_grad = jnp.einsum("rd,rf->df", normed, packed_grad, preferred_element_type=jnp.float32)
    qkv_bias_grad = jnp.sum(packed_grad.astype(jnp.float32), 0)
    first_grad = jnp.einsum(
        "rf,df->rd", packed_grad, attn_back[2], preferred_element_type=jnp.float32
    )
    first_pull = jax.vjp(
        layer_norm, inputs, attn_back[0].astype(jnp.float32), attn_back[1].astype(jnp.float32)
    )[1]
    input_part, ln1_gain_grad, ln1_bias_grad = first_pull(first_grad)
    input_grad = middle_grad + input_part
    attn_grads = (
        lax.psum_scatter(ln1_gain_grad, ("dp", "fsdp"), scatter_dimension=0, tiled=True),
        lax.psum_scatter(ln1_bias_grad, ("dp", "fsdp"), scatter_dimension=0, tiled=True),
        lax.psum_scatter(qkv_grad, ("dp", "fsdp"), scatter_dimension=0, tiled=True),
        lax.psum_scatter(qkv_bias_grad, ("dp", "fsdp"), scatter_dimension=0, tiled=True),
        lax.psum_scatter(out_grad, ("dp", "fsdp"), scatter_dimension=0, tiled=True),
        lax.psum_scatter(out_bias_grad, ("dp", "fsdp"), scatter_dimension=0, tiled=True),
    )
    gradients = tuple(attn_grads) + tuple(mlp_grads)
    return (
        output,
        input_grad,
        gradients[0],
        gradients[1],
        gradients[2],
        gradients[3],
        gradients[4],
        gradients[5],
        gradients[6],
        gradients[7],
        gradients[8],
        gradients[9],
        gradients[10],
        gradients[11],
    )


def solution(mesh):
    placed = (
        P(("dp", "fsdp"), None),
        P(("dp", "fsdp")),
        P(("dp", "fsdp")),
        P(("dp", "fsdp")),
        P(("dp", "fsdp"), None),
        P(("dp", "fsdp")),
        P(("dp", "fsdp"), None),
        P(("dp", "fsdp")),
        P(("dp", "fsdp")),
        P(("dp", "fsdp")),
        P(("dp", "fsdp"), None),
        P(("dp", "fsdp")),
        P(("dp", "fsdp"), None),
        P(("dp", "fsdp")),
        P(("dp", "fsdp"), None),
    )
    return jax.shard_map(
        on_device,
        mesh=mesh,
        in_specs=placed,
        out_specs=(
            P(("dp", "fsdp"), None),
            P(("dp", "fsdp"), None),
            P(("dp", "fsdp")),
            P(("dp", "fsdp")),
            P(("dp", "fsdp"), None),
            P(("dp", "fsdp")),
            P(("dp", "fsdp"), None),
            P(("dp", "fsdp")),
            P(("dp", "fsdp")),
            P(("dp", "fsdp")),
            P(("dp", "fsdp"), None),
            P(("dp", "fsdp")),
            P(("dp", "fsdp"), None),
            P(("dp", "fsdp")),
        ),
        check_vma=False,
    )
```

profile of v0, /device:TPU:0, one launch (start us, length us, event | category | flops | bytes accessed | tf_op | source)
XLA Modules:
  0.0 917.2 jit_solution(26999538219399620)
XLA Ops:
  16.2 43.0 %all-reduce.17 = (bf16[2304]{0:T(1024)(128)(2,1)S(1)}, bf16[768]{0:T(1024)(128)(2,1)S(1)}, bf16[768]{0:T(1024)(128)(2,1)S(1)}, bf16[768]{0:T(1024)(128)(2,1)S(1)...) all-reduce(bf16[2304]{0:T(1024)(128)(2,1)S(1)} %dynamic-update-slic, ...), channel_id=1, replica_groups=mesh['dp'=4,'fsdp'=8] {'dp','fsdp'}, use_global_device_ids=true, to_apply=%add.2 | all-reduce | flops 9984 | bytes 39936
  62.7 11.3 %all-gather.5.cloned.1.call-done = bf16[768,2304]{1,0:T(8,128)(2,1)} async-done(((bf16[24,2304]{1,0:T(8,128)(2,1)}), bf16[768,2304]{1,0:T(8,128)(2,1)}) %all-gather.5.cloned.1.call-update) | async-done | bytes 3538960 | tf_op jit(solution)/shard_map/all_gather | solution.py:145
  87.8 30.9 %collective-permute-done.1 = bf16[512]{0:T(512)(128)(2,1)S(1)} collective-permute-done((bf16[512]{0:T(512)(128)(2,1)S(1)}, bf16[512]{0:T(512)(128)(2,1)S(1)}, u32[]{:S(2)}, u32[]{:S(2)}) %collective-permute-start.1) | collective-permute-done | bytes 1056 | tf_op jit(solution)/shard_map/ppermute | solution.py:16
  129.5 75.0 %while.36 = (s32[]{:T(128)}, bf16[3,512,4,64]{1,3,2,0:T(8,128)(2,1)}, bf16[3,1024,4,64]{1,3,2,0:T(8,128)(2,1)}, bf16[3,512,4,64]{1,3,2,0:T(8,128)(2,1)S(1)}, bf1...) while((s32[]{:T(128)}, bf16[3,512,4,64]{1,3,2,0:T(8,128)(2,1)}, ...), condition=%wide.region_5.6_spmd, body=%wide.region_2.5_spmd.sunk | while | flops 1109394432 | bytes 21254228 | solution.py:98
  129.9 14.0 %fusion.216 = (f32[4,512]{1,0:T(4,128)S(1)}, f32[4,512,1024]{2,1,0:T(8,128)}) fusion(pred[512,1024]{1,0:T(8,128)(4,1)S(1)} %get-tuple-element.405, bf16[3,1024,4,64]{1,3,2,0:T(8,128)(2,1)S(1)} %get-tuple-element.404, s32[]{:T(128)S(6)} %copy.57, bf16[3,512,4,64]{1,3,2,0:T(8,128)(2,1)S(1)} %get-tuple-element.403), kind=kOutput, calls=%fused_computation.174.clone.1 | convolution fusion | flops 557843456 | bytes 11020288 | tf_op jit(solution)/shard_map/while/body/eval_jaxpr/sub | solution.py:44
  143.9 10.9 %fusion.217 = bf16[3,512,4,64]{1,3,2,0:T(8,128)(2,1)} fusion(bf16[3,512,4,64]{1,3,2,0:T(8,128)(2,1)} %get-tuple-element.394, s32[]{:T(128)S(6)} %copy.57, f32[4,512,1024]{2,1,0:T(8,128)} %get-tuple-element.365, f32[4,512]{1,0:T(4,128)S(1)} %get-tuple-element.366, bf16[3,1024,4,64]{1,3,2,0:T(8,128)(2,1)} %get-tuple-element.402, ...), kind=kOutput, calls=%fused_computation.13.clone.1 | convolution fusion | flops 551550976 | bytes 10233856 | tf_op jit(solution)/shard_map/while/body/eval_jaxpr/hrk,khe->rhe/dot_general | solution.py:47
  154.8 13.9 %fusion.216 = (f32[4,512]{1,0:T(4,128)S(1)}, f32[4,512,1024]{2,1,0:T(8,128)}) fusion(pred[512,1024]{1,0:T(8,128)(4,1)S(1)} %get-tuple-element.405, bf16[3,1024,4,64]{1,3,2,0:T(8,128)(2,1)S(1)} %get-tuple-element.404, s32[]{:T(128)S(6)} %copy.57, bf16[3,512,4,64]{1,3,2,0:T(8,128)(2,1)S(1)} %get-tuple-element.403), kind=kOutput, calls=%fused_computation.174.clone.1 | convolution fusion | flops 557843456 | bytes 11020288 | tf_op jit(solution)/shard_map/while/body/eval_jaxpr/sub | solution.py:44
  168.7 10.9 %fusion.217 = bf16[3,512,4,64]{1,3,2,0:T(8,128)(2,1)} fusion(bf16[3,512,4,64]{1,3,2,0:T(8,128)(2,1)} %get-tuple-element.394, s32[]{:T(128)S(6)} %copy.57, f32[4,512,1024]{2,1,0:T(8,128)} %get-tuple-element.365, f32[4,512]{1,0:T(4,128)S(1)} %get-tuple-element.366, bf16[3,1024,4,64]{1,3,2,0:T(8,128)(2,1)} %get-tuple-element.402, ...), kind=kOutput, calls=%fused_computation.13.clone.1 | convolution fusion | flops 551550976 | bytes 10233856 | tf_op jit(solution)/shard_map/while/body/eval_jaxpr/hrk,khe->rhe/dot_general | solution.py:47
  179.6 13.9 %fusion.216 = (f32[4,512]{1,0:T(4,128)S(1)}, f32[4,512,1024]{2,1,0:T(8,128)}) fusion(pred[512,1024]{1,0:T(8,128)(4,1)S(1)} %get-tuple-element.405, bf16[3,1024,4,64]{1,3,2,0:T(8,128)(2,1)S(1)} %get-tuple-element.404, s32[]{:T(128)S(6)} %copy.57, bf16[3,512,4,64]{1,3,2,0:T(8,128)(2,1)S(1)} %get-tuple-element.403), kind=kOutput, calls=%fused_computation.174.clone.1 | convolution fusion | flops 557843456 | bytes 11020288 | tf_op jit(solution)/shard_map/while/body/eval_jaxpr/sub | solution.py:44
  193.5 11.0 %fusion.217 = bf16[3,512,4,64]{1,3,2,0:T(8,128)(2,1)} fusion(bf16[3,512,4,64]{1,3,2,0:T(8,128)(2,1)} %get-tuple-element.394, s32[]{:T(128)S(6)} %copy.57, f32[4,512,1024]{2,1,0:T(8,128)} %get-tuple-element.365, f32[4,512]{1,0:T(4,128)S(1)} %get-tuple-element.366, bf16[3,1024,4,64]{1,3,2,0:T(8,128)(2,1)} %get-tuple-element.402, ...), kind=kOutput, calls=%fused_computation.13.clone.1 | convolution fusion | flops 551550976 | bytes 10233856 | tf_op jit(solution)/shard_map/while/body/eval_jaxpr/hrk,khe->rhe/dot_general | solution.py:47
  209.6 62.1 %while.37 = (s32[]{:T(128)}, bf16[3,512,4,64]{1,3,2,0:T(8,128)(2,1)}, f32[3,4,512]{2,1,0:T(4,128)S(1)}, bf16[3,1024,4,64]{1,3,2,0:T(8,128)(2,1)}, bf16[3,512,4,6...) while((s32[]{:T(128)}, ...), condition=%wide.region_13.14_spmd, body=%wide.region_10.13_spmd.sunk | while | flops 578811904 | bytes 34932888 | solution.py:98
  279.9 9.8 %convert_reduce_fusion = (f32[3072]{0:T(1024)}, bf16[512,3072]{1,0:T(8,128)(2,1)S(1)}) fusion(f32[512,3072]{1,0:T(8,128)} %fusion.138, f32[3072]{0:T(1024)S(1)} %copy-done.36, bf16[512,768]{1,0:T(8,128)(2,1)} %param.35, bf16[3072,768]{1,0:T(8,128)(2,1)} %all-gather.11.cloned.1.call-done), kind=kOutput, calls=%fused_computation.107 | convolution fusion | flops 2452091904 | bytes 14966784 | tf_op jit(solution)/shard_map/rd,fd->rf/dot_general | solution.py:181
  305.8 151.5 %while.38 = (s32[]{:T(128)}, bf16[3,512,4,64]{1,3,2,0:T(8,128)(2,1)}, f32[3,1024,4,64]{1,3,2,0:T(8,128)}, f32[3,1024,4,64]{1,3,2,0:T(8,128)}, bf16[3,1024,4,64]{...) while((s32[]{:T(128)}, ...), condition=%wide.region_16.17_spmd, body=%wide.region_14.16_spmd.sunk | while | flops 1409682432 | bytes 100701384 | solution.py:225
  316.5 26.1 %fusion.234 = bf16[4,512,1024]{2,1,0:T(8,128)(2,1)S(1)} fusion(f32[4,512,1024]{2,1,0:T(8,128)} %fusion.232, f32[4,512,1024]{2,1,0:T(8,128)} %fusion.233, f32[4,512]{1,0:T(4,128)S(1)} %dynamic-slice_bitcast_fusion.2, pred[512,1024]{1,0:T(8,128)(4,1)S(1)} %get-tuple-element.458), kind=kOutput, calls=%fused_computation.65.clone.1 | output fusion | flops 50334720 | bytes 21504000 | tf_op jit(solution)/shard_map/while/body/eval_jaxpr/sub | solution.py:61
  366.9 26.1 %fusion.234 = bf16[4,512,1024]{2,1,0:T(8,128)(2,1)S(1)} fusion(f32[4,512,1024]{2,1,0:T(8,128)} %fusion.232, f32[4,512,1024]{2,1,0:T(8,128)} %fusion.233, f32[4,512]{1,0:T(4,128)S(1)} %dynamic-slice_bitcast_fusion.2, pred[512,1024]{1,0:T(8,128)(4,1)S(1)} %get-tuple-element.458), kind=kOutput, calls=%fused_computation.65.clone.1 | output fusion | flops 50334720 | bytes 21504000 | tf_op jit(solution)/shard_map/while/body/eval_jaxpr/sub | solution.py:61
  417.1 26.1 %fusion.234 = bf16[4,512,1024]{2,1,0:T(8,128)(2,1)S(1)} fusion(f32[4,512,1024]{2,1,0:T(8,128)} %fusion.232, f32[4,512,1024]{2,1,0:T(8,128)} %fusion.233, f32[4,512]{1,0:T(4,128)S(1)} %dynamic-slice_bitcast_fusion.2, pred[512,1024]{1,0:T(8,128)(4,1)S(1)} %get-tuple-element.458), kind=kOutput, calls=%fused_computation.65.clone.1 | output fusion | flops 50334720 | bytes 21504000 | tf_op jit(solution)/shard_map/while/body/eval_jaxpr/sub | solution.py:61
  448.5 8.4 fusion.237
  462.6 36.9 %collective-permute-done.2 = bf16[512,1536]{0,1:T(8,128)(2,1)S(1)} collective-permute-done((bf16[512,1536]{0,1:T(8,128)(2,1)S(1)}, bf16[512,1536]{0,1:T(8,128)(2,1)S(1)}, u32[]{:S(2)}, u32[]{:S(2)}) %collective-permute-start.2) | collective-permute-done | bytes 1572896 | tf_op jit(solution)/shard_map/ppermute | solution.py:16
  516.3 10.3 %fusion.140 = f32[3072,768]{1,0:T(8,128)} fusion(bf16[512,768]{1,0:T(8,128)(2,1)S(1)} %copy-done.10, f32[512,3072]{1,0:T(8,128)} %fusion.138, f32[3072]{0:T(1024)S(1)} %copy-done.37), kind=kOutput, calls=%fused_computation.171 | convolution fusion | flops 2431647744 | bytes 16527360 | tf_op jit(solution)/shard_map/rf,rd->fd/dot_general | solution.py:179
  527.3 9.5 %add_convert_fusion = bf16[512,768]{1,0:T(8,128)(2,1)} fusion(f32[512,768]{1,0:T(8,128)S(1)} %copy-done.6, bf16[3072,768]{1,0:T(8,128)(2,1)} %all-gather.11.cloned.1.call-done, f32[768]{0:T(1024)S(1)} %convert_element_type.126, f32[512,3072]{1,0:T(8,128)} %fusion.138, f32[3072]{0:T(1024)S(1)} %copy-done.37), kind=kOutput, calls=%fused_computation.143 | convolution fusion | flops 2432827392 | bytes 13384704 | tf_op jit(solution)/shard_map/dot_general | solution.py:115
  543.8 42.7 %all-reduce.16 = (f32[768]{0:T(1024)S(1)}, f32[768]{0:T(1024)S(1)}, f32[2304]{0:T(1024)S(1)}, f32[768]{0:T(1024)S(1)}, f32[768]{0:T(1024)S(1)}, /*index=5*/f32[7...) all-reduce(f32[768]{0:T(1024)S(1)} %get-tuple-element.146, ...), channel_id=2, replica_groups=mesh['dp'=4,'fsdp'=8] {'dp','fsdp'}, use_global_device_ids=true, to_apply=%region_20.21.clone | all-reduce | flops 9984 | bytes 79872
  591.3 35.6 %reduce-scatter.5.cloned.1.call-done = f32[24,2304]{1,0:T(8,128)} async-done(((f32[768,2304]{1,0:T(8,128)}), f32[24,2304]{1,0:T(8,128)}) %reduce-scatter.5.cloned.1.call-update) | async-done | bytes 221200 | tf_op jit(solution)/shard_map/reduce_scatter | solution.py:254
  626.9 141.2 %reduce-scatter.9.cloned.1.call-done = f32[24,3072]{1,0:T(8,128)} async-done(((f32[768,3072]{1,0:T(8,128)}), f32[24,3072]{1,0:T(8,128)}) %reduce-scatter.9.cloned.1.call-update) | async-done | bytes 294928 | tf_op jit(solution)/shard_map/reduce_scatter | solution.py:199
  768.0 142.1 %reduce-scatter.11.cloned.1.call-done = f32[96,768]{1,0:T(8,128)} async-done(((f32[3072,768]{1,0:T(8,128)}), f32[96,768]{1,0:T(8,128)}) %reduce-scatter.11.cloned.1.call-update) | async-done | bytes 294928 | tf_op jit(solution)/shard_map/reduce_scatter | solution.py:201
  (258 shorter events, 225.8 us)
Async XLA Ops:
  7.2 66.7 %all-gather.5.cloned.1.call-start = ((), (), s32[]{:S(2)}) async-start(), calls=%async_computation.4 | async-start | bytes 3649536 | tf_op jit(solution)/shard_map/all_gather | solution.py:145
  7.9 196.6 %all-gather.7.cloned.1.call-start = ((), (), s32[]{:S(2)}) async-start(), calls=%async_computation.5 | async-start | bytes 1216512 | tf_op jit(solution)/shard_map/all_gather | solution.py:147
  8.7 263.0 %all-gather.9.cloned.1.call-start = ((), (), s32[]{:S(2)}) async-start(), calls=%async_computation.6 | async-start | bytes 4866048 | tf_op jit(solution)/shard_map/all_gather | solution.py:162
  9.4 270.5 %all-gather.11.cloned.1.call-start = ((), (), s32[]{:S(2)}) async-start(), calls=%async_computation.7 | async-start | bytes 4866048 | tf_op jit(solution)/shard_map/all_gather | solution.py:164
  59.2 19.1 %copy-start.43 = (f32[768]{0:T(1024)}, f32[768]{0:T(1024)S(1)}, u32[]{:S(2)}) copy-start(f32[768]{0:T(1024)S(1)} %convert_element_type.112) | copy-start | bytes 9220
  59.2 19.1 %copy-start.20 = (f32[768]{0:T(1024)}, f32[768]{0:T(1024)S(1)}, u32[]{:S(2)}) copy-start(f32[768]{0:T(1024)S(1)} %convert_element_type.111) | copy-start | bytes 9220
  60.6 17.8 %copy-start.22 = (f32[512]{0:T(512)}, f32[512]{0:T(512)S(1)}, u32[]{:S(2)}) copy-start(f32[512]{0:T(512)S(1)} %broadcast_multiply_fusion.1) | copy-start | bytes 6148
  62.7 15.7 %copy-start.26 = (f32[512]{0:T(512)}, f32[512]{0:T(512)S(1)}, u32[]{:S(2)}) copy-start(f32[512]{0:T(512)S(1)} %fusion.130) | copy-start | bytes 6148
  79.6 42.4 %collective-permute-start = (bf16[512,1536]{1,0:T(8,128)(2,1)}, bf16[512,1536]{1,0:T(8,128)(2,1)}, u32[]{:S(2)}, u32[]{:S(2)}) collective-permute-start(bf16[512,1536]{1,0:T(8,128)(2,1)} %slice.64), channel_id=1, source_target_pairs={{0,1},{1,2},{2,3},{3,4},{4,5},{5,6},{6,7},{8,9},{9,10},{10,11},{11... | collective-permute-start | bytes 4718600 | tf_op jit(solution)/shard_map/ppermute | solution.py:16
  84.1 34.6 %collective-permute-start.1 = (bf16[512]{0:T(512)(128)(2,1)S(1)}, bf16[512]{0:T(512)(128)(2,1)S(1)}, u32[]{:S(2)}, u32[]{:S(2)}) collective-permute-start(bf16[512]{0:T(512)(128)(2,1)S(1)} %convert_element_type.116), channel_id=1, source_target_pairs={{0,1},{1,2},{2,3},{3,4},{4,5},{5,6},{6,7},{8,9},{9,10},{10,11},{11... | collective-permute-start | bytes 3080 | tf_op jit(solution)/shard_map/ppermute | solution.py:16
  85.9 505.4 %reduce-scatter.7.cloned.1.call-start = ((), (), s32[]{:S(2)}) async-start(), calls=%async_computation.9 | async-start | bytes 2433024 | tf_op jit(solution)/shard_map/reduce_scatter | solution.py:256
  207.2 86.2 %copy-start.28 = (f32[512]{0:T(512)}, f32[512]{0:T(512)S(1)}, u32[]{:S(2)}) copy-start(f32[512]{0:T(512)S(1)} %broadcast_multiply_fusion) | copy-start | bytes 6148
  208.6 84.7 %copy-start.39 = (f32[512]{0:T(512)}, f32[512]{0:T(512)S(1)}, u32[]{:S(2)}) copy-start(f32[512]{0:T(512)S(1)} %fusion.131) | copy-start | bytes 6148
  209.6 62.1 %copy-start.34 = (f32[768]{0:T(1024)S(1)}, f32[768]{0:T(1024)}, u32[]{:S(2)}) copy-start(f32[768]{0:T(1024)} %convert_element_type.121) | copy-start | bytes 9220
  209.6 62.1 %copy-start.45 = (f32[768]{0:T(1024)S(1)}, f32[768]{0:T(1024)}, u32[]{:S(2)}) copy-start(f32[768]{0:T(1024)} %convert_element_type.122) | copy-start | bytes 9220
  279.9 9.8 %copy-start.49 = (bf16[768,3072]{1,0:T(8,128)(2,1)S(1)}, bf16[768,3072]{1,0:T(8,128)(2,1)}, u32[]{:S(2)}) copy-start(bf16[768,3072]{1,0:T(8,128)(2,1)} %all-gather.9.cloned.1.call-done) | copy-start | bytes 14155780
  304.8 322.0 %reduce-scatter.5.cloned.1.call-start = ((), (), s32[]{:S(2)}) async-start(), calls=%async_computation.8 | async-start | bytes 7299072 | tf_op jit(solution)/shard_map/reduce_scatter | solution.py:254
  306.0 10.5 %copy-start.1 = (bf16[3,512,4,64]{1,3,2,0:T(8,128)(2,1)}, bf16[3,512,4,64]{1,3,2,0:T(8,128)(2,1)S(1)}, u32[]{:S(2)}) copy-start(bf16[3,512,4,64]{1,3,2,0:T(8,128)(2,1)S(1)} %get-tuple-element.459) | copy-start | bytes 2359300 | tf_op jit(solution)/shard_map/while
  356.4 10.5 %copy-start.1 = (bf16[3,512,4,64]{1,3,2,0:T(8,128)(2,1)}, bf16[3,512,4,64]{1,3,2,0:T(8,128)(2,1)S(1)}, u32[]{:S(2)}) copy-start(bf16[3,512,4,64]{1,3,2,0:T(8,128)(2,1)S(1)} %get-tuple-element.459) | copy-start | bytes 2359300 | tf_op jit(solution)/shard_map/while
  406.7 10.5 %copy-start.1 = (bf16[3,512,4,64]{1,3,2,0:T(8,128)(2,1)}, bf16[3,512,4,64]{1,3,2,0:T(8,128)(2,1)S(1)}, u32[]{:S(2)}) copy-start(bf16[3,512,4,64]{1,3,2,0:T(8,128)(2,1)S(1)} %get-tuple-element.459) | copy-start | bytes 2359300 | tf_op jit(solution)/shard_map/while
  460.7 38.8 %collective-permute-start.2 = (bf16[512,1536]{0,1:T(8,128)(2,1)S(1)}, bf16[512,1536]{0,1:T(8,128)(2,1)S(1)}, u32[]{:S(2)}, u32[]{:S(2)}) collective-permute-start(bf16[512,1536]{0,1:T(8,128)(2,1)S(1)} %pad_maximum_fusion.3), channel_id=1, source_target_pairs={{1,0},{2,1},{3,2},{4,3},{5,4},{6,5},{7,6},{9,8},{10,9},{11,10},{12... | collective-permute-start | bytes 4718600 | tf_op jit(solution)/shard_map/ppermute | solution.py:16
  506.6 261.5 %reduce-scatter.9.cloned.1.call-start = ((), (), s32[]{:S(2)}) async-start(), calls=%async_computation.10 | async-start | bytes 9732096 | tf_op jit(solution)/shard_map/reduce_scatter | solution.py:199
  515.2 395.0 %reduce-scatter.11.cloned.1.call-start = ((), (), s32[]{:S(2)}) async-start(), calls=%async_computation.11 | async-start | bytes 9732096 | tf_op jit(solution)/shard_map/reduce_scatter | solution.py:201
  527.3 9.9 %copy-start.50 = (bf16[768,2304]{1,0:T(8,128)(2,1)S(1)}, bf16[768,2304]{1,0:T(8,128)(2,1)}, u32[]{:S(2)}) copy-start(bf16[768,2304]{1,0:T(8,128)(2,1)} %all-gather.5.cloned.1.call-done) | copy-start | bytes 10616836
  (50 other events, 176.5 us)
Sparse Core Ops, SparseCore 0:
  11.0 62.8 all-gather.4
  76.9 56.1 all-gather.6
  136.1 62.6 all-gather.8
  201.6 62.5 all-gather.10
  304.9 100.8 reduce-scatter.6
  506.7 120.1 reduce-scatter.4
  633.3 134.6 reduce-scatter.8
  775.5 134.6 reduce-scatter.10
where the time goes:
time: 924 us; the launch traced here: 917 us
  waiting for transfers between devices  400 us (43%)
  matrix products  258 us (28%)
  other arithmetic  110 us (12%)
  blocking collectives  85.8 us (9%)
  local copies, waits for them, and re-layouts  37.9 us (4%)
  between operations  15 us (2%)
    reduce_scatter x1, waiting for transfers between devices, on_device(): lax.psum_scatter(fc2_grad, ('dp', 'fsdp'), scatter_dimension=0, tiled=True)  142 us
    reduce_scatter x1, waiting for transfers between devices, on_device(): lax.psum_scatter(fc1_grad, ('dp', 'fsdp'), scatter_dimension=0, tiled=True)  141 us
    unnamed x2, blocking collectives  85.8 us
    sub x3, other arithmetic, backward_tile(): signs * weight_grad - centre  78.3 us
    ppermute x3, waiting for transfers between devices, from_behind(): return lax.ppermute(block, axis, route)  67.8 us
    dot_general x6, matrix products, forward_tile(): jnp.einsum('hrk,khe->rhe', attention, value_rows, preferred_element_type=...  56.2 us
    sub x3, matrix products, forward_tile(): raised = jnp.where(allowed, jnp.exp(magnitude - row_max), 0.0)  41.8 us
    reduce_scatter x1, waiting for transfers between devices, on_device(): lax.psum_scatter(qkv_grad, ('dp', 'fsdp'), scatter_dimension=0, tiled=True)  35.6 us
  transfers between devices with their start and end apart: 11, of which 6 were waited for; matrix products, arithmetic and copies ran while one was open for 41% of the time, Pallas kernels for 0%

commit v1 on v0

v1 whole, which is shorter than its diff:
```python
import functools

import jax
import jax.numpy as jnp
from jax import lax
from jax.experimental import pallas as pl
from jax.experimental.pallas import tpu as pltpu
from jax.sharding import Mesh, PartitionSpec as P

D = 768
HEAD = 64
PAIR = 2 * HEAD
EPSILON = 1e-05
NEG = -1e30
TILE = 256
BF = jnp.bfloat16
F32 = jnp.float32
MIB = 1 << 20


def nn(a, b):
    return jnp.dot(a, b, preferred_element_type=F32)


def nt(a, b):
    return lax.dot_general(a, b, (((1,), (1,)), ((), ())), preferred_element_type=F32)


def tn(a, b):
    return lax.dot_general(a, b, (((0,), (0,)), ((), ())), preferred_element_type=F32)


def normalise(rows):
    average = jnp.mean(rows, -1, keepdims=True)
    centred = rows - average
    inverse = lax.rsqrt(jnp.mean(centred * centred, -1, keepdims=True) + EPSILON)
    return centred * inverse, inverse


def norm_grad(grad, hat, inverse, gain):
    scaled = grad * gain
    return inverse * (
        scaled
        - jnp.mean(scaled, -1, keepdims=True)
        - hat * jnp.mean(scaled * hat, -1, keepdims=True)
    )


def total(rows):
    return jnp.sum(rows, 0, keepdims=True)


def project_kernel(place_ref, own_ref, other_ref, gain_ref, shift_ref, weight_ref, bias_ref, normed_ref, qkv_ref):
    mine = (pl.program_id(0) // 2) == place_ref[0]
    rows = jnp.where(mine, own_ref[...].astype(F32), other_ref[...].astype(F32))
    hat, _ = normalise(rows)
    normed = (hat * gain_ref[...] + shift_ref[...]).astype(BF)
    normed_ref[...] = normed
    qkv_ref[...] = (nn(normed, weight_ref[...]) + bias_ref[...]).astype(BF)


def project(place, own, other, gain, shift, weight, bias):
    rows, width = own.shape
    columns = weight.shape[1]
    step = rows // 2
    half = pl.BlockSpec((step, width), lambda i, s: (i % 2, 0))
    fixed = lambda r, c: pl.BlockSpec((r, c), lambda i, s: (0, 0))
    return pl.pallas_call(
        project_kernel,
        grid_spec=pltpu.PrefetchScalarGridSpec(
            num_scalar_prefetch=1,
            grid=(4,),
            in_specs=[half, half, fixed(1, width), fixed(1, width), fixed(width, columns), fixed(1, columns)],
            out_specs=[
                pl.BlockSpec((step, width), lambda i, s: (i, 0)),
                pl.BlockSpec((step, columns), lambda i, s: (i, 0)),
            ],
        ),
        out_shape=[
            jax.ShapeDtypeStruct((2 * rows, width), BF),
            jax.ShapeDtypeStruct((2 * rows, columns), BF),
        ],
        compiler_params=pltpu.CompilerParams(vmem_limit_bytes=48 * MIB),
        cost_estimate=pl.CostEstimate(
            flops=4 * rows * width * columns, bytes_accessed=8 * MIB, transcendentals=0
        ),
        name="norm_and_qkv",
    )(place, own, other, gain, shift, weight, bias)


def forward_kernel(q_ref, k_ref, v_ref, first_ref, o_ref, lse_ref, mag_buf, sign_buf):
    count = q_ref.shape[0] // TILE
    lane = lax.broadcasted_iota(jnp.int32, (1, PAIR), 1)
    values = jnp.transpose(v_ref[...].astype(F32)).astype(BF)
    key_at = lax.broadcasted_iota(jnp.int32, (TILE, TILE), 0)
    causal = key_at <= lax.broadcasted_iota(jnp.int32, (TILE, TILE), 1)
    for j in range(count):
        qs = slice(j * TILE, (j + 1) * TILE)
        q = q_ref[qs, :] * BF(HEAD**-0.5)
        first = first_ref[:, qs]
        heads = []
        for h in range(2):
            qh = jnp.where((lane >= HEAD) == (h == 1), q, BF(0))
            top = None
            for i in range(j + 1):
                ks = slice(i * TILE, (i + 1) * TILE)
                s = nt(k_ref[ks, :], qh)
                square = s * s + 1.0
                inverse = lax.rsqrt(square)
                allowed = key_at + i * TILE >= first
                if i == j:
                    allowed = allowed & causal
                mag = jnp.where(allowed, square * inverse, NEG)
                mag_buf[h, ks, :] = mag
                sign_buf[h, ks, :] = s * inverse
                best = jnp.max(mag, 0, keepdims=True)
                top = best if top is None else jnp.maximum(top, best)
            weight_sum = jnp.zeros((1, TILE), F32)
            mixture = jnp.zeros((HEAD, TILE), F32)
            for i in range(j + 1):
                ks = slice(i * TILE, (i + 1) * TILE)
                raised = jnp.exp(mag_buf[h, ks, :] - top)
                weight_sum = weight_sum + total(raised)
                mixture = mixture + nn(
                    values[h * HEAD : (h + 1) * HEAD, ks], (sign_buf[h, ks, :] * raised).astype(BF)
                )
            heads.append(mixture * (1.0 / weight_sum))
            lse_ref[0, h : h + 1, qs] = top + jnp.log(weight_sum)
        o_ref[qs, :] = jnp.transpose(jnp.concatenate(heads, 0)).astype(BF)


def attend(qkv, firsts):
    length, columns = qkv.shape
    pairs = columns // 3 // PAIR
    block = lambda part: pl.BlockSpec((length, PAIR), lambda p: (0, part * pairs + p))
    return pl.pallas_call(
        forward_kernel,
        grid=(pairs,),
        in_specs=[block(0), block(1), block(2), pl.BlockSpec((1, length), lambda p: (0, 0))],
        out_specs=[block(0), pl.BlockSpec((1, 2, length), lambda p: (p, 0, 0))],
        out_shape=[
            jax.ShapeDtypeStruct((length, columns // 3), BF),
            jax.ShapeDtypeStruct((pairs, 2, length), F32),
        ],
        scratch_shapes=[pltpu.VMEM((2, length, TILE), F32)] * 2,
        compiler_params=pltpu.CompilerParams(vmem_limit_bytes=48 * MIB),
        cost_estimate=pl.CostEstimate(
            flops=12 * MIB * 1024, bytes_accessed=4 * MIB, transcendentals=0
        ),
        name="attention_forward",
    )(qkv, qkv, qkv, firsts)


def backward_kernel(
    q_ref, k_ref, v_ref, do_ref, lse_ref, first_ref, dq_ref, dk_ref, dv_ref, dk_sum, dv_sum, part_buf, weight_buf
):
    count = q_ref.shape[0] // TILE
    lane = lax.broadcasted_iota(jnp.int32, (1, PAIR), 1)
    keys = jnp.transpose(k_ref[...].astype(F32)).astype(BF)
    key_at = lax.broadcasted_iota(jnp.int32, (TILE, TILE), 0)
    causal = key_at <= lax.broadcasted_iota(jnp.int32, (TILE, TILE), 1)
    for j in range(count):
        qs = slice(j * TILE, (j + 1) * TILE)
        q = q_ref[qs, :] * BF(HEAD**-0.5)
        do = do_ref[qs, :]
        first = first_ref[:, qs]
        heads = []
        for h in range(2):
            chosen = (lane >= HEAD) == (h == 1)
            qh = jnp.where(chosen, q, BF(0))
            doh = jnp.where(chosen, do, BF(0))
            lse = lse_ref[0, h : h + 1, qs]
            centre = jnp.zeros((1, TILE), F32)
            for i in range(j + 1):
                ks = slice(i * TILE, (i + 1) * TILE)
                s = nt(k_ref[ks, :], qh)
                dw = nt(v_ref[ks, :], doh)
                square = s * s + 1.0
                inverse = lax.rsqrt(square)
                allowed = key_at + i * TILE >= first
                if i == j:
                    allowed = allowed & causal
                p = jnp.exp(jnp.where(allowed, square * inverse - lse, NEG))
                w = s * inverse * p
                centre = centre + total(w * dw)
                part_buf[h, ks, :] = p * dw * (1.0 + inverse * inverse * (inverse - 1.0))
                weight_buf[h, ks, :] = w
                dv = nn(w.astype(BF), doh)
                if i == j and h == 0:
                    dv_sum[ks, :] = dv
                else:
                    dv_sum[ks, :] += dv
            dq = jnp.zeros((HEAD, TILE), F32)
            for i in range(j + 1):
                ks = slice(i * TILE, (i + 1) * TILE)
                ds = (part_buf[h, ks, :] - weight_buf[h, ks, :] * centre).astype(BF)
                dk = nn(ds, qh)
                if i == j and h == 0:
                    dk_sum[ks, :] = dk
                else:
                    dk_sum[ks, :] += dk
                dq = dq + nn(keys[h * HEAD : (h + 1) * HEAD, ks], ds)
            heads.append(dq)
        dq_ref[qs, :] = (jnp.transpose(jnp.concatenate(heads, 0)) * HEAD**-0.5).astype(BF)
    dk_ref[...] = dk_sum[...].astype(BF)
    dv_ref[...] = dv_sum[...].astype(BF)


def attend_back(qkv, do, lse, firsts):
    length, columns = qkv.shape
    pairs = columns // 3 // PAIR
    block = lambda part: pl.BlockSpec((length, PAIR), lambda p: (0, part * pairs + p))
    shape = jax.ShapeDtypeStruct((length, columns // 3), BF)
    return pl.pallas_call(
        backward_kernel,
        grid=(pairs,),
        in_specs=[
            block(0),
            block(1),
            block(2),
            block(0),
            pl.BlockSpec((1, 2, length), lambda p: (p, 0, 0)),
            pl.BlockSpec((1, length), lambda p: (0, 0)),
        ],
        out_specs=[block(0)] * 3,
        out_shape=[shape] * 3,
        scratch_shapes=[pltpu.VMEM((length, PAIR), F32)] * 2 + [pltpu.VMEM((2, length, TILE), F32)] * 2,
        compiler_params=pltpu.CompilerParams(vmem_limit_bytes=48 * MIB),
        cost_estimate=pl.CostEstimate(
            flops=24 * MIB * 1024, bytes_accessed=6 * MIB, transcendentals=0
        ),
        name="attention_backward",
    )(qkv, qkv, qkv, do, lse, firsts)


FF_STEP = 768
OUT_BIAS, GAIN, SHIFT, LAST_BIAS = range(4)
D_OUT_BIAS, D_GAIN, D_SHIFT, D_LAST_BIAS = range(4)


def middle_kernel(
    tok_ref, o_ref, g_ref, wo_ref, w1_ref, w2_ref, b1_ref, vec_ref,
    out_ref, dx_ref, do_ref, gone_ref, gtwo_ref, db1_ref, sums_ref,
    x_buf, h_buf, y_sum, dh_sum,
):
    step = pl.program_id(0)
    last = pl.num_programs(0) - 1

    @pl.when(step == 0)
    def _():
        x = tok_ref[...].astype(F32) + nn(o_ref[...], wo_ref[...]) + vec_ref[OUT_BIAS : OUT_BIAS + 1, :]
        x_buf[...] = x
        hat, _ = normalise(x)
        h_buf[...] = (hat * vec_ref[GAIN : GAIN + 1, :] + vec_ref[SHIFT : SHIFT + 1, :]).astype(BF)
        y_sum[...] = jnp.zeros_like(y_sum)
        dh_sum[...] = jnp.zeros_like(dh_sum)

    @pl.when(step < last)
    def _():
        h = h_buf[...]
        g = g_ref[...]
        u = nn(h, w1_ref[...]) + b1_ref[...]
        root = 0.7978845608028654
        u2 = u * u
        bent = jnp.tanh(root * u * (1.0 + 0.044715 * u2))
        a = (0.5 * u * (1.0 + bent)).astype(BF)
        slope = 0.5 * (1.0 + bent) + 0.5 * u * (1.0 - bent * bent) * (root * (1.0 + 0.134145 * u2))
        y_sum[...] += nn(a, w2_ref[...])
        du = (nt(g, w2_ref[...]) * slope).astype(BF)
        db1_ref[...] = total(du.astype(F32))
        dh_sum[...] += nt(du, w1_ref[...])
        gone_ref[...] = tn(h, du).astype(BF)
        gtwo_ref[...] = tn(a, g).astype(BF)

    @pl.when(step == last)
    def _():
        x = x_buf[...]
        g = g_ref[...].astype(F32)
        out_ref[...] = (x + y_sum[...] + vec_ref[LAST_BIAS : LAST_BIAS + 1, :]).astype(BF)
        hat, inverse = normalise(x)
        dh = dh_sum[...]
        dx = g + norm_grad(dh, hat, inverse, vec_ref[GAIN : GAIN + 1, :])
        dx_ref[...] = dx
        dxr = dx.astype(BF)
        do_ref[...] = nt(dxr, wo_ref[...]).astype(BF)
        gone_ref[...] = tn(o_ref[...], dxr).astype(BF)
        sums_ref[...] = jnp.zeros_like(sums_ref)
        sums_ref[D_OUT_BIAS : D_OUT_BIAS + 1, :] = total(dx)
        sums_ref[D_GAIN : D_GAIN + 1, :] = total(dh * hat)
        sums_ref[D_SHIFT : D_SHIFT + 1, :] = total(dh)
        sums_ref[D_LAST_BIAS : D_LAST_BIAS + 1, :] = total(g)


def middle(tokens, mixture, grad, wo, w1, w2, b1, vectors):
    rows, width = tokens.shape
    hidden = w1.shape[1]
    steps = hidden // FF_STEP
    fixed = lambda r, c: pl.BlockSpec((r, c), lambda i: (0, 0))
    across = lambda r: pl.BlockSpec((r, FF_STEP), lambda i: (0, jnp.minimum(i, steps - 1)))
    down = pl.BlockSpec((FF_STEP, width), lambda i: (jnp.minimum(i, steps - 1), 0))
    return pl.pallas_call(
        middle_kernel,
        grid=(steps + 1,),
        in_specs=[
            fixed(rows, width), fixed(rows, width), fixed(rows, width), fixed(width, width),
            across(width), down, across(1), fixed(*vectors.shape),
        ],
        out_specs=[
            fixed(rows, width), fixed(rows, width), fixed(rows, width),
            pl.BlockSpec((width, FF_STEP), lambda i: (0, i)), down, across(1), fixed(8, width),
        ],
        out_shape=[
            jax.ShapeDtypeStruct((rows, width), BF),
            jax.ShapeDtypeStruct((rows, width), F32),
            jax.ShapeDtypeStruct((rows, width), BF),
            jax.ShapeDtypeStruct((width, hidden + FF_STEP), BF),
            jax.ShapeDtypeStruct((hidden, width), BF),
            jax.ShapeDtypeStruct((1, hidden), F32),
            jax.ShapeDtypeStruct((8, width), F32),
        ],
        scratch_shapes=[
            pltpu.VMEM((rows, width), F32),
            pltpu.VMEM((rows, width), BF),
            pltpu.VMEM((rows, width), F32),
            pltpu.VMEM((rows, width), F32),
        ],
        compiler_params=pltpu.CompilerParams(vmem_limit_bytes=56 * MIB),
        cost_estimate=pl.CostEstimate(
            flops=12 * rows * width * (hidden + width // 2), bytes_accessed=30 * MIB, transcendentals=0
        ),
        name="feed_forward_both_ways",
    )(tokens, mixture, grad, wo, w1, w2, b1, vectors)


def unproject_kernel(
    place_ref, own_ref, other_ref, dq_ref, dk_ref, dv_ref, weight_ref, keep_ref, send_ref, sums_ref, bias_ref
):
    step = pl.program_id(0)
    mine = (step // 2) == place_ref[0]
    rows = jnp.where(mine, own_ref[...].astype(F32), other_ref[...].astype(F32))
    hat, _ = normalise(rows)
    third = dq_ref.shape[1]
    grad = nt(dq_ref[...], weight_ref[:, :third])
    grad = grad + nt(dk_ref[...], weight_ref[:, third : 2 * third])
    grad = grad + nt(dv_ref[...], weight_ref[:, 2 * third :])

    @pl.when(step == 0)
    def _():
        sums_ref[...] = jnp.zeros_like(sums_ref)
        bias_ref[...] = jnp.zeros_like(bias_ref)

    sums_ref[0:1, :] += total(grad * hat)
    sums_ref[1:2, :] += total(grad)
    bias_ref[0:1, :] += total(dq_ref[...].astype(F32))
    bias_ref[1:2, :] += total(dk_ref[...].astype(F32))
    bias_ref[2:3, :] += total(dv_ref[...].astype(F32))

    @pl.when(mine)
    def _():
        keep_ref[...] = grad

    @pl.when(jnp.logical_not(mine))
    def _():
        send_ref[...] = grad.astype(BF)


def unproject(place, own, other, dq, dk, dv, weight):
    rows, width = own.shape
    third = dq.shape[1]
    step = rows // 2
    half = pl.BlockSpec((step, width), lambda i, s: (i % 2, 0))
    part = pl.BlockSpec((step, third), lambda i, s: (i, 0))
    fixed = lambda r, c: pl.BlockSpec((r, c), lambda i, s: (0, 0))
    return pl.pallas_call(
        unproject_kernel,
        grid_spec=pltpu.PrefetchScalarGridSpec(
            num_scalar_prefetch=1,
            grid=(4,),
            in_specs=[half, half, part, part, part, fixed(*weight.shape)],
            out_specs=[
                pl.BlockSpec((step, width), lambda i, s: (jnp.clip(i - 2 * s[0], 0, 1), 0)),
                pl.BlockSpec((step, width), lambda i, s: (jnp.clip(i - 2 * (1 - s[0]), 0, 1), 0)),
                fixed(8, width),
                fixed(8, third),
            ],
        ),
        out_shape=[
            jax.ShapeDtypeStruct((rows, width), F32),
            jax.ShapeDtypeStruct((rows, width), BF),
            jax.ShapeDtypeStruct((8, width), F32),
            jax.ShapeDtypeStruct((8, third), F32),
        ],
        compiler_params=pltpu.CompilerParams(vmem_limit_bytes=48 * MIB),
        cost_estimate=pl.CostEstimate(
            flops=12 * rows * width * third, bytes_accessed=10 * MIB, transcendentals=0
        ),
        name="grad_at_first_norm",
    )(place, own, other, dq, dk, dv, weight)


def swap(block, axis):
    return lax.ppermute(block, axis, [(0, 1), (1, 0)])


def on_device(
    tokens, segment_ids, ln1_gain, ln1_bias, qkv_weight, qkv_bias, out_weight, out_bias,
    ln2_gain, ln2_bias, fc1_weight, fc1_bias, fc2_weight, fc2_bias, output_grad,
):
    outer, inner = lax.axis_size("outer"), lax.axis_size("inner")
    core, side = lax.axis_index("core"), lax.axis_index("side")
    everyone = ("outer", "core", "inner", "side")
    chips = ("outer", "inner", "side")
    rows = tokens.shape[0]
    share = qkv_weight.shape[0]
    place = side.astype(jnp.int32).reshape(1)

    other = swap(tokens, "side")
    other_marks = swap(segment_ids, "side")
    marks = jnp.where(
        side == 0,
        jnp.concatenate([segment_ids, other_marks]),
        jnp.concatenate([other_marks, segment_ids]),
    )
    firsts = sum(jnp.where(marks > v, jnp.sum(marks == v), 0) for v in range(3))
    firsts = firsts.astype(jnp.int32)[None, :]

    parts = qkv_weight.reshape(share, 3, 2, D // 2).transpose(2, 0, 1, 3).reshape(2, share, 3 * D // 2)
    vectors = jnp.concatenate(
        [
            v.reshape(share, -1)
            for v in (ln1_gain, ln1_bias, qkv_bias, out_bias, ln2_gain, ln2_bias, fc1_bias, fc2_bias)
        ],
        1,
    )
    vectors = jnp.pad(vectors, ((0, 0), (0, 128 - vectors.shape[1])))
    parts = jnp.concatenate([parts, jnp.broadcast_to(vectors, (2, share, 128))], 2)
    parts = parts.reshape(2, share, 2, 5 * 128).transpose(2, 0, 1, 3)
    parts = jnp.broadcast_to(parts[None, :, None], (outer, 2, inner, 2, share, 5 * 128))
    got = lax.all_to_all(
        parts.reshape(outer * inner * 4, share, 5 * 128), everyone, split_axis=0, concat_axis=0, tiled=True
    ).reshape(D, 5 * 128)
    twin = swap(got, "core")
    packed = jnp.where(core == 0, jnp.concatenate([got, twin], 1), jnp.concatenate([twin, got], 1))
    w_qkv = packed[:, : 9 * 128]
    table = packed[:, 9 * 128 :].astype(F32)
    column = lambda i: table[:, i][None, :]
    qkv_bias_all = table[:, 2:5].reshape(3, 2, D // 2)
    qkv_bias_mine = lax.dynamic_index_in_dim(qkv_bias_all, side, 1, keepdims=False).reshape(1, -1)
    b1 = table[:, 8:12].reshape(1, -1)
    mid_vectors = jnp.concatenate([column(5), column(6), column(7), column(12)], 0)

    wide = lax.all_gather(jnp.concatenate([fc1_weight, out_weight], 1), everyone, axis=0, tiled=True)
    w2 = lax.all_gather(fc2_weight, everyone, axis=0, tiled=True)
    w1, wo = wide[:, : fc1_weight.shape[1]], wide[:, fc1_weight.shape[1] :]

    normed, qkv = project(place, tokens, other, column(0), column(1), w_qkv, qkv_bias_mine)
    mixed, lse = attend(qkv, firsts)
    theirs = lax.dynamic_slice_in_dim(mixed, (1 - side) * rows, rows, 0)
    mine = lax.dynamic_slice_in_dim(mixed, side * rows, rows, 0)
    theirs = swap(theirs, "side")
    mixture = jnp.where(side == 0, jnp.concatenate([mine, theirs], 1), jnp.concatenate([theirs, mine], 1))

    output, dx1, do, grad_wide, grad_two, db1, sums = middle(
        tokens, mixture, output_grad, wo, w1, w2, b1, mid_vectors
    )

    half = D // 2
    do_mine = lax.dynamic_slice_in_dim(do, side * half, half, 1)
    do_theirs = swap(lax.dynamic_slice_in_dim(do, (1 - side) * half, half, 1), "side")
    do_all = jnp.where(side == 0, jnp.concatenate([do_mine, do_theirs]), jnp.concatenate([do_theirs, do_mine]))

    def reduce_rows(grad):
        width = grad.shape[1]
        pieces = grad.reshape(outer, 2, inner * 2, grad.shape[0] // (4 * outer * inner), width)
        keep = lax.dynamic_index_in_dim(pieces, core, 1, keepdims=False)
        send = lax.dynamic_index_in_dim(pieces, 1 - core, 1, keepdims=False)
        both = (keep.astype(F32) + swap(send, "core").astype(F32)).astype(BF)
        both = both.reshape((outer * inner * 2,) + both.shape[2:])
        return lax.all_to_all(both, chips, split_axis=0, concat_axis=0, tiled=True)

    wide_total = jnp.sum(reduce_rows(grad_wide).astype(F32), 0)
    two_total = jnp.sum(reduce_rows(grad_two).astype(F32), 0)

    dq, dk, dv = attend_back(qkv, do_all, lse, firsts)
    kept, sent, first_sums, bias_sums = unproject(place, tokens, other, dq, dk, dv, w_qkv)
    back = swap(sent, "side")
    grad_qkv = jnp.concatenate([tn(normed, d).astype(BF) for d in (dq, dk, dv)], 1)
    bias_mine = jnp.zeros((3, 2, half), F32)
    bias_mine = lax.dynamic_update_slice(bias_mine, bias_sums[:3][:, None], (0, side, 0)).reshape(-1)
    small = jnp.concatenate(
        [
            v.reshape(D, -1)
            for v in (
                first_sums[0], first_sums[1], bias_mine, sums[D_OUT_BIAS], sums[D_GAIN],
                sums[D_SHIFT], db1, sums[D_LAST_BIAS],
            )
        ],
        1,
    )
    small = jnp.pad(small, ((0, 0), (0, 128 - small.shape[1]))).astype(BF)
    tail = reduce_rows(jnp.concatenate([grad_qkv, small], 1)).astype(F32)
    tail = tail.reshape(outer * inner, 2, share, 10 * 128)
    qkv_total = jnp.sum(tail[..., : 9 * 128], 0).reshape(2, share, 3, half)
    qkv_total = qkv_total.transpose(1, 2, 0, 3).reshape(share, 3 * D)
    small_total = jnp.sum(tail[..., 9 * 128 :], (0, 1))
    pick = lambda i, n=1: small_total[:, i : i + n].reshape(-1)

    hat, inverse = normalise(tokens.astype(F32))
    input_grad = dx1 + norm_grad(kept + back.astype(F32), hat, inverse, column(0))
    hidden = fc1_weight.shape[1]
    return (
        output,
        input_grad,
        pick(0),
        pick(1),
        qkv_total,
        pick(2, 3),
        wide_total[:, hidden:],
        pick(5),
        pick(6),
        pick(7),
        wide_total[:, :hidden],
        pick(8, 4),
        two_total,
        pick(12),
    )


def solution(mesh):
    dp, fsdp = mesh.devices.shape
    finer = Mesh(
        mesh.devices.reshape(dp // 2, 2, fsdp // 2, 2), ("outer", "core", "inner", "side")
    )
    every = ("outer", "core", "inner", "side")
    vec, mat = P(every), P(every, None)
    return jax.shard_map(
        on_device,
        mesh=finer,
        in_specs=(mat, vec, vec, vec, mat, vec, mat, vec, vec, vec, mat, vec, mat, vec, mat),
        out_specs=(mat, mat, vec, vec, mat, vec, mat, vec, vec, vec, mat, vec, mat, vec),
        check_vma=False,
    )
```

time: 924 us -> 419 us (0.45)
  matrix products: 258 us -> 3.28 us
  waiting for transfers between devices: 400 us -> 186 us
  other arithmetic: 110 us -> 30.1 us
  Pallas kernels: 0 us -> 71 us
  blocking collectives: 85.8 us -> 44.4 us
  starting transfers between devices: 8.27 us -> 21.6 us
    reduce_scatter x4 -> x0, waiting for transfers between devices: 319 us -> none  [the longest x1 142 us: on_device(): lax.psum_scatter(fc2_grad, ('dp', 'fsdp'), scatter_dimension=0, tiled=True)]
    dot_general x36 -> x3, matrix products: 216 us -> 3.28 us  [tn(): lax.dot_general(a, b, (((0,), (0,)), ((), ())), preferred_element_type=F32)]
    unnamed x2 -> x0, blocking collectives: 85.8 us -> none
    sub x3 -> x0, other arithmetic: 78.3 us -> none  [backward_tile(): signs * weight_grad - centre]
    all_to_all x0 -> x3, waiting for transfers between devices: none -> 72.6 us  [reduce_rows(): return lax.all_to_all(both, chips, split_axis=0, concat_axis=0, tiled=True)]
    pallas_call x0 -> x5, Pallas kernels: none -> 71 us  [the longest x1 27.2 us: middle(): pl.pallas_call(middle_kernel, grid=(steps + 1,), in_specs=[fixed(rows, wi...]
    all_to_all x0 -> x1, blocking collectives: none -> 44.4 us  [on_device(): lax.all_to_all(parts.reshape(outer * inner * 4, share, 5 * 128), everyone...]
    sub x3 -> x0, matrix products: 41.8 us -> none  [forward_tile(): raised = jnp.where(allowed, jnp.exp(magnitude - row_max), 0.0)]
  transfers between devices with their start and end apart: 11 -> 14, of which waited for: 6 -> 10; matrix products, arithmetic and copies ran while one was open for 41% -> 13% of each run, Pallas kernels for 0% -> 4%
where the time goes in v1:
time: 419 us; the launch traced here: 417 us
  waiting for transfers between devices  186 us (44%)
  Pallas kernels  71 us (17%)
  local copies, waits for them, and re-layouts  46.5 us (11%)
  blocking collectives  44.4 us (11%)
  other arithmetic  30.1 us (7%)
  starting transfers between devices  21.6 us (5%)
  between operations  14.5 us (3%)
    ppermute x9, waiting for transfers between devices, swap(): return lax.ppermute(block, axis, [(0, 1), (1, 0)])  80.1 us
    all_to_all x3, waiting for transfers between devices, reduce_rows(): return lax.all_to_all(both, chips, split_axis=0, concat_axis=0, tiled=True)  72.6 us
    all_to_all x1, blocking collectives, on_device(): lax.all_to_all(parts.reshape(outer * inner * 4, share, 5 * 128), everyone...  44.4 us
    all_gather x1, waiting for transfers between devices, on_device(): w2 = lax.all_gather(fc2_weight, everyone, axis=0, tiled=True)  32.2 us
    pallas_call x1, Pallas kernels, middle(): pl.pallas_call(middle_kernel, grid=(steps + 1,), in_specs=[fixed(rows, wi...  27.2 us
    pallas_call x1, Pallas kernels, attend_back(): pl.pallas_call(backward_kernel, grid=(pairs,), in_specs=[block(0), block(...  19.9 us
    all_to_all x3, starting transfers between devices, reduce_rows(): return lax.all_to_all(both, chips, split_axis=0, concat_axis=0, tiled=True)  13.9 us
    pallas_call x1, Pallas kernels, attend(): pl.pallas_call(forward_kernel, grid=(pairs,), in_specs=[block(0), block(1...  12.7 us
  transfers between devices with their start and end apart: 14, of which 10 were waited for; matrix products, arithmetic and copies ran while one was open for 13% of the time, Pallas kernels for 4%

profile of v1, /device:TPU:0, one launch (start us, length us, event | category | flops | bytes accessed | tf_op | source)
XLA Modules:
  0.0 417.1 jit_solution(2109986473777734329)
XLA Ops:
  17.1 44.4 %all_to_all.20 = bf16[32,24,640]{2,1,0:T(8,128)(2,1)S(1)} all-to-all(bf16[32,24,640]{2,1,0:T(8,128)(2,1)S(1)} %bitcast.71), channel_id=1, replica_groups=mesh['outer'=2,'core'=2,'inner'=4,'side'=2] {'outer','core','inner','side'}, dimensions={0} | all-to-all | bytes 1966080 | tf_op jit(solution)/shard_map/all_to_all | solution.py:439
  71.5 3.2 slice_reduce_fusion.4
  74.7 17.5 %collective-permute-done.other_ref = bf16[512,768]{1,0:T(8,128)(2,1)S(1)} collective-permute-done((bf16[512,768]{1,0:T(8,128)(2,1)S(1)}, bf16[512,768]{1,0:T(8,128)(2,1)S(1)}, u32[]{:S(2)}, u32[]{:S(2)}) %collective-permute-start) | collective-permute-done | bytes 786464 | tf_op jit(solution)/shard_map/ppermute | solution.py:402
  92.2 4.6 %norm_and_qkv.1 = (bf16[1024,768]{1,0:T(8,128)(2,1)S(1)}, bf16[1024,1152]{1,0:T(8,128)(2,1)}) custom-call(s32[1]{0:T(128)} %bitcast.place_ref, bf16[512,768]{1,0:T(8,128)(2,1)S(1)} %copy-done, bf16[512,768]{1,0:T(8,128)(2,1)S(1)} %collective-permute-done.other_ref, f32[1,768]{1,0:T(1,128)S(1)} %broadcast_in_dim_squeeze.19.gain_ref, ...), custom_call_target="tpu_custom_call" | custom-call | flops 1811939328 | bytes 8388608 | tf_op jit(solution)/shard_map/norm_and_qkv/pallas_call | solution.py:68
  99.7 12.7 %attention_forward.1 = (bf16[1024,384]{1,0:T(8,128)(2,1)S(1)}, f32[3,2,1024]{2,1,0:T(2,128)S(1)}) custom-call(bf16[1024,1152]{1,0:T(8,128)(2,1)S(1)} %copy-done.5, bf16[1024,1152]{1,0:T(8,128)(2,1)S(1)} %copy-done.5, bf16[1024,1152]{1,0:T(8,128)(2,1)S(1)} %copy-done.5, s32[1,1024]{1,0:T(1,128)S(1)} %fusion.16.first_ref), custom_call_target="tpu_custom_call" | custom-call | flops 12884901888 | bytes 4194304 | tf_op jit(solution)/shard_map/attention_forward/pallas_call | solution.py:136
  115.8 7.4 %collective-permute-done.3 = bf16[512,384]{1,0:T(8,128)(2,1)S(1)} collective-permute-done((bf16[512,384]{1,0:T(8,128)(2,1)S(1)}, bf16[512,384]{1,0:T(8,128)(2,1)S(1)}, u32[]{:S(2)}, u32[]{:S(2)}) %collective-permute-start.3) | collective-permute-done | bytes 393248 | tf_op jit(solution)/shard_map/ppermute | solution.py:402
  124.2 4.9 %slice.137.w1_ref = bf16[768,3072]{1,0:T(8,128)(2,1)} slice(bf16[768,3840]{1,0:T(8,128)(2,1)} %all-gather.3.cloned.1.call-done), slice={[0:768], [0:3072]} | slice | bytes 9437184 | tf_op jit(solution)/shard_map/slice | solution.py:454
  131.5 32.2 %all-gather.5.cloned.1.call-done.w2_ref = bf16[3072,768]{1,0:T(8,128)(2,1)} async-done(((bf16[96,768]{1,0:T(8,128)(2,1)}), bf16[3072,768]{1,0:T(8,128)(2,1)}) %all-gather.5.cloned.1.call-update) | async-done | bytes 4718608 | tf_op jit(solution)/shard_map/all_gather | solution.py:453
  163.7 27.2 %feed_forward_both_ways.1 = (bf16[512,768]{1,0:T(8,128)(2,1)}, f32[512,768]{1,0:T(8,128)}, bf16[512,768]{1,0:T(8,128)(2,1)}, bf16[768,3840]{1,0:T(8,128)(2,1)}, ...) custom-call(bf16[512,768]{1,0:T(8,128)(2,1)} %own_ref.3, ...), custom_call_target="tpu_custom_call" | custom-call | flops 16307453952 | bytes 31457280 | tf_op jit(solution)/shard_map/feed_forward_both_ways/pallas_call | solution.py:301
  196.2 7.2 %collective-permute-done.4 = bf16[512,384]{1,0:T(8,128)(2,1)S(1)} collective-permute-done((bf16[512,384]{1,0:T(8,128)(2,1)S(1)}, bf16[512,384]{1,0:T(8,128)(2,1)S(1)}, u32[]{:S(2)}, u32[]{:S(2)}) %collective-permute-start.4) | collective-permute-done | bytes 393248 | tf_op jit(solution)/shard_map/ppermute | solution.py:402
  205.4 19.9 %attention_backward.1 = (bf16[1024,384]{1,0:T(8,128)(2,1)S(1)}, bf16[1024,384]{1,0:T(8,128)(2,1)S(1)}, bf16[1024,384]{1,0:T(8,128)(2,1)S(1)}) custom-call(bf16[1024,1152]{1,0:T(8,128)(2,1)S(1)} %copy-done.6, bf16[1024,1152]{1,0:T(8,128)(2,1)S(1)} %copy-done.6, bf16[1024,1152]{1,0:T(8,128)(2,1)S(1)} %copy-done.6, ...), custom_call_target="tpu_custom_call" | custom-call | flops 25769803776 | bytes 6291456 | tf_op jit(solution)/shard_map/attention_backward/pallas_call | solution.py:214
  228.7 6.7 %grad_at_first_norm.1 = (f32[512,768]{1,0:T(8,128)}, bf16[512,768]{1,0:T(8,128)(2,1)S(1)}, f32[8,768]{1,0:T(8,128)S(1)}, f32[8,384]{1,0:T(8,128)S(1)}) custom-call(s32[1]{0:T(128)} %bitcast.place_ref, bf16[512,768]{1,0:T(8,128)(2,1)S(1)} %copy-done.1, bf16[512,768]{1,0:T(8,128)(2,1)S(1)} %collective-permute-done.other_ref, ...), custom_call_target="tpu_custom_call" | custom-call | flops 1811939328 | bytes 10485760 | tf_op jit(solution)/shard_map/grad_at_first_norm/pallas_call | solution.py:374
  239.2 4.0 copy.91
  245.4 3.2 dynamic-slice_bitcast_fusion.1
  251.5 4.4 %all-to-all-start.1 = ((bf16[16,24,1280]{2,1,0:T(8,128)(2,1)}), bf16[16,24,1280]{2,1,0:T(8,128)(2,1)S(1)}, u32[]{:S(2)}, u32[]{:S(2)}) async-start(bf16[16,24,1280]{2,1,0:T(8,128)(2,1)} %bitcast.70), calls=%async_computation.1 | async-start | bytes 1966080 | tf_op jit(solution)/shard_map/all_to_all | solution.py:479
  256.0 4.5 %fusion.1 = bf16[2,8,96,768]{3,2,1,0:T(8,128)(2,1)} fusion(bf16[2,8,96,768]{3,2,1,0:T(8,128)(2,1)} %collective-permute-done.8, bf16[2,2,8,96,768]{4,3,2,1,0:T(8,128)(2,1)} %bitcast.69, s32[]{:T(128)S(6)} %select_n.122), kind=kLoop, calls=%fused_computation.4 | loop fusion | flops 4718592 | bytes 7077892 | tf_op jit(solution)/shard_map/convert_element_type | solution.py:477
  260.5 20.1 %all-to-all-done.1 = bf16[16,24,1280]{2,1,0:T(8,128)(2,1)S(1)} async-done(((bf16[16,24,1280]{2,1,0:T(8,128)(2,1)}), bf16[16,24,1280]{2,1,0:T(8,128)(2,1)S(1)}, u32[]{:S(2)}, u32[]{:S(2)}) %all-to-all-start.1) | async-done | bytes 983072 | tf_op jit(solution)/shard_map/all_to_all | solution.py:479
  280.6 4.5 %all-to-all-start.3 = ((bf16[16,96,768]{2,1,0:T(8,128)(2,1)}), bf16[16,96,768]{2,1,0:T(8,128)(2,1)}, u32[]{:S(2)}, u32[]{:S(2)}) async-start(bf16[16,96,768]{2,1,0:T(8,128)(2,1)} %bitcast.63), calls=%async_computation.3 | async-start | bytes 4718592 | tf_op jit(solution)/shard_map/all_to_all | solution.py:479
  287.2 5.4 %collective-permute-done.7 = bf16[2,8,24,3840]{3,2,1,0:T(8,128)(2,1)S(1)} collective-permute-done((bf16[2,8,24,3840]{3,2,1,0:T(8,128)(2,1)S(1)}, bf16[2,8,24,3840]{3,2,1,0:T(8,128)(2,1)S(1)}, u32[]{:S(2)}, u32[]{:S(2)}) %collective-permute-start.7) | collective-permute-done | bytes 2949152 | tf_op jit(solution)/shard_map/ppermute | solution.py:402
  292.5 4.2 %fusion = bf16[2,8,24,3840]{3,2,1,0:T(8,128)(2,1)} fusion(bf16[2,8,24,3840]{3,2,1,0:T(8,128)(2,1)S(1)} %collective-permute-done.7, bf16[2,2,8,24,3840]{4,3,2,1,0:T(8,128)(2,1)} %bitcast.67, s32[]{:T(128)S(6)} %select_n.122), kind=kLoop, calls=%fused_computation.1 | loop fusion | flops 5898240 | bytes 8847364 | tf_op jit(solution)/shard_map/convert_element_type | solution.py:477
  296.7 40.9 %all-to-all-done.3 = bf16[16,96,768]{2,1,0:T(8,128)(2,1)} async-done(((bf16[16,96,768]{2,1,0:T(8,128)(2,1)}), bf16[16,96,768]{2,1,0:T(8,128)(2,1)}, u32[]{:S(2)}, u32[]{:S(2)}) %all-to-all-start.3) | async-done | bytes 2359328 | tf_op jit(solution)/shard_map/all_to_all | solution.py:479
  337.7 5.0 %all-to-all-start.2 = ((bf16[16,24,3840]{2,1,0:T(8,128)(2,1)}), bf16[16,24,3840]{2,1,0:T(8,128)(2,1)}, u32[]{:S(2)}, u32[]{:S(2)}) async-start(bf16[16,24,3840]{2,1,0:T(8,128)(2,1)} %bitcast.62), calls=%async_computation.2 | async-start | bytes 5898240 | tf_op jit(solution)/shard_map/all_to_all | solution.py:479
  345.2 41.1 %collective-permute-done.5 = bf16[512,768]{1,0:T(8,128)(2,1)S(1)} collective-permute-done((bf16[512,768]{1,0:T(8,128)(2,1)S(1)}, bf16[512,768]{1,0:T(8,128)(2,1)S(1)}, u32[]{:S(2)}, u32[]{:S(2)}) %collective-permute-start.5) | collective-permute-done | bytes 786464 | tf_op jit(solution)/shard_map/ppermute | solution.py:402
  395.0 11.6 %all-to-all-done.2 = bf16[16,24,3840]{2,1,0:T(8,128)(2,1)} async-done(((bf16[16,24,3840]{2,1,0:T(8,128)(2,1)}), bf16[16,24,3840]{2,1,0:T(8,128)(2,1)}, u32[]{:S(2)}, u32[]{:S(2)}) %all-to-all-start.2) | async-done | bytes 2949152 | tf_op jit(solution)/shard_map/all_to_all | solution.py:479
  (125 shorter events, 65.9 us)
Async XLA Ops:
  7.2 117.1 %all-gather.3.cloned.1.call-start = ((), (), s32[]{:S(2)}) async-start(), calls=%async_computation.4 | async-start | bytes 6082560 | tf_op jit(solution)/shard_map/all_gather | solution.py:452
  8.9 154.9 %all-gather.5.cloned.1.call-start = ((), (), s32[]{:S(2)}) async-start(), calls=%async_computation.5 | async-start | bytes 4866048 | tf_op jit(solution)/shard_map/all_gather | solution.py:453
  13.7 47.9 %copy-start.11 = (s32[512]{0:T(512)S(1)}, s32[512]{0:T(512)}, u32[]{:S(2)}) copy-start(s32[512]{0:T(512)} %param.16) | copy-start | bytes 6148
  13.7 48.5 %copy-start = (bf16[512,768]{1,0:T(8,128)(2,1)S(1)}, bf16[512,768]{1,0:T(8,128)(2,1)}, u32[]{:S(2)}) copy-start(bf16[512,768]{1,0:T(8,128)(2,1)} %own_ref.3) | copy-start | bytes 2359300
  61.6 6.2 %collective-permute-start.1 = (bf16[768,640]{1,0:T(8,128)(2,1)S(1)}, bf16[768,640]{1,0:T(8,128)(2,1)S(1)}, u32[]{:S(2)}, u32[]{:S(2)}) collective-permute-start(bf16[768,640]{1,0:T(8,128)(2,1)S(1)} %bitcast.72), channel_id=1, source_target_pairs={{0,8},{8,0},{1,9},{9,1},{2,10},{10,2},{3,11},{11,3},{4,12},{12,4},... | collective-permute-start | bytes 2949128 | tf_op jit(solution)/shard_map/ppermute | solution.py:402
  61.6 3.6 collective-permute-start.2
  62.2 30.0 %collective-permute-start = (bf16[512,768]{1,0:T(8,128)(2,1)S(1)}, bf16[512,768]{1,0:T(8,128)(2,1)S(1)}, u32[]{:S(2)}, u32[]{:S(2)}) collective-permute-start(bf16[512,768]{1,0:T(8,128)(2,1)S(1)} %copy-done), channel_id=1, source_target_pairs={{0,1},{1,0},{2,3},{3,2},{4,5},{5,4},{6,7},{7,6},{8,9},{9,8},{10,11... | collective-permute-start | bytes 2359304 | tf_op jit(solution)/shard_map/ppermute | solution.py:402
  68.5 23.8 %copy-start.2 = (bf16[768,1152]{1,0:T(8,128)(2,1)}, bf16[768,1152]{1,0:T(8,128)(2,1)S(1)}, u32[]{:S(2)}) copy-start(bf16[768,1152]{1,0:T(8,128)(2,1)S(1)} %slice.134.weight_ref) | copy-start | bytes 5308420
  98.0 1.7 copy-start.5
  99.7 14.4 %copy-start.8 = (f32[768,128]{1,0:T(8,128)S(1)}, f32[768,128]{1,0:T(8,128)}, u32[]{:S(2)}) copy-start(f32[768,128]{1,0:T(8,128)} %copy-done.7) | copy-start | bytes 1179652
  112.5 10.7 %collective-permute-start.3 = (bf16[512,384]{1,0:T(8,128)(2,1)S(1)}, bf16[512,384]{1,0:T(8,128)(2,1)S(1)}, u32[]{:S(2)}, u32[]{:S(2)}) collective-permute-start(bf16[512,384]{1,0:T(8,128)(2,1)S(1)} %get-tuple-element.70), channel_id=1, source_target_pairs={{0,1},{1,0},{2,3},{3,2},{4,5},{5,4},{6,7},{7,6},{8,9},{9,8},{10,11... | collective-permute-start | bytes 1179656 | tf_op jit(solution)/shard_map/ppermute | solution.py:402
  192.1 11.4 %collective-permute-start.4 = (bf16[512,384]{1,0:T(8,128)(2,1)S(1)}, bf16[512,384]{1,0:T(8,128)(2,1)S(1)}, u32[]{:S(2)}, u32[]{:S(2)}) collective-permute-start(bf16[512,384]{1,0:T(8,128)(2,1)S(1)} %get-tuple-element.68), channel_id=1, source_target_pairs={{0,1},{1,0},{2,3},{3,2},{4,5},{5,4},{6,7},{7,6},{8,9},{9,8},{10,11... | collective-permute-start | bytes 1179656 | tf_op jit(solution)/shard_map/ppermute | solution.py:402
  203.8 1.7 copy-start.6
  205.4 19.9 %copy-start.4 = (bf16[1024,768]{1,0:T(8,128)(2,1)S(1)}, bf16[1024,768]{1,0:T(8,128)(2,1)}, u32[]{:S(2)}) copy-start(bf16[1024,768]{1,0:T(8,128)(2,1)} %copy-done.3) | copy-start | bytes 4718596
  227.0 1.7 copy-start.1
  245.4 3.7 collective-permute-start.6
  248.6 7.3 %collective-permute-start.8 = (bf16[2,8,96,768]{3,2,1,0:T(8,128)(2,1)}, bf16[2,8,96,768]{3,2,1,0:T(8,128)(2,1)}, u32[]{:S(2)}, u32[]{:S(2)}) collective-permute-start(bf16[2,8,96,768]{3,2,1,0:T(8,128)(2,1)} %dynamic-slice_bitcast_fusion.1), channel_id=1, source_target_pairs={{0,8},{8,0},{1,9},{9,1},{2,10},{10,2},{3,11},{11,3},{4,12},{12,4},... | collective-permute-start | bytes 7077896 | tf_op jit(solution)/shard_map/ppermute | solution.py:402
  251.5 29.1 %all-to-all-start.1 = ((bf16[16,24,1280]{2,1,0:T(8,128)(2,1)}), bf16[16,24,1280]{2,1,0:T(8,128)(2,1)S(1)}, u32[]{:S(2)}, u32[]{:S(2)}) async-start(bf16[16,24,1280]{2,1,0:T(8,128)(2,1)} %bitcast.70), calls=%async_computation.1 | async-start | bytes 1966080 | tf_op jit(solution)/shard_map/all_to_all | solution.py:479
  280.6 57.1 %all-to-all-start.3 = ((bf16[16,96,768]{2,1,0:T(8,128)(2,1)}), bf16[16,96,768]{2,1,0:T(8,128)(2,1)}, u32[]{:S(2)}, u32[]{:S(2)}) async-start(bf16[16,96,768]{2,1,0:T(8,128)(2,1)} %bitcast.63), calls=%async_computation.3 | async-start | bytes 4718592 | tf_op jit(solution)/shard_map/all_to_all | solution.py:479
  287.1 5.4 %collective-permute-start.7 = (bf16[2,8,24,3840]{3,2,1,0:T(8,128)(2,1)S(1)}, bf16[2,8,24,3840]{3,2,1,0:T(8,128)(2,1)S(1)}, u32[]{:S(2)}, u32[]{:S(2)}) collective-permute-start(bf16[2,8,24,3840]{3,2,1,0:T(8,128)(2,1)S(1)} %dynamic-slice_bitcast_fusion), channel_id=1, source_target_pairs={{0,8},{8,0},{1,9},{9,1},{2,10},{10,2},{3,11},{11,3},{4,12},{12,4},... | collective-permute-start | bytes 8847368 | tf_op jit(solution)/shard_map/ppermute | solution.py:402
  337.7 68.9 %all-to-all-start.2 = ((bf16[16,24,3840]{2,1,0:T(8,128)(2,1)}), bf16[16,24,3840]{2,1,0:T(8,128)(2,1)}, u32[]{:S(2)}, u32[]{:S(2)}) async-start(bf16[16,24,3840]{2,1,0:T(8,128)(2,1)} %bitcast.62), calls=%async_computation.2 | async-start | bytes 5898240 | tf_op jit(solution)/shard_map/all_to_all | solution.py:479
  342.7 43.6 %copy-start.9 = (f32[512,768]{1,0:T(8,128)S(1)}, f32[512,768]{1,0:T(8,128)}, u32[]{:S(2)}) copy-start(f32[512,768]{1,0:T(8,128)} %get-tuple-element.41) | copy-start | bytes 4718596
  342.7 43.6 %collective-permute-start.5 = (bf16[512,768]{1,0:T(8,128)(2,1)S(1)}, bf16[512,768]{1,0:T(8,128)(2,1)S(1)}, u32[]{:S(2)}, u32[]{:S(2)}) collective-permute-start(bf16[512,768]{1,0:T(8,128)(2,1)S(1)} %get-tuple-element.42), channel_id=1, source_target_pairs={{0,1},{1,0},{2,3},{3,2},{4,5},{5,4},{6,7},{7,6},{8,9},{9,8},{10,11... | collective-permute-start | bytes 2359304 | tf_op jit(solution)/shard_map/ppermute | solution.py:402
  344.8 42.1 %copy-start.10 = (f32[512,768]{1,0:T(8,128)S(1)}, f32[512,768]{1,0:T(8,128)}, u32[]{:S(2)}) copy-start(f32[512,768]{1,0:T(8,128)} %get-tuple-element.35) | copy-start | bytes 4718596
  (2 other events, 2.0 us)
Sparse Core Ops, SparseCore 0:
  11.6 86.7 all-gather.2
  101.4 62.3 all-gather.4
